TPU v7x, 32 devices: a whole 2x2x4 slice. The times are simulated.
32 devices in a mesh: expert: 4 (over y, x), req: 8 (over z, core).
Axes of the slice: x: 2, y: 2, z: 4, core: 2. Of those that a mesh axis runs over, the one named last changes fastest.
Arguments:
- queries: bfloat16 [8192, 1024], P(('expert', 'req')), may hold values from -82 to 82
- self_kv: bfloat16 [8192, 2048], P(('expert', 'req')), may hold values from -4 to 4
- kv_pages: bfloat16 [32, 128, 2048], P(('expert', 'req')), may hold values from -4 to 4
- page_table: int32 [4, 8], P('expert'), may hold values from 0 to 7, as said below
- lengths: int32 [8192], P(('expert', 'req')), may hold values from 1 to 1024
- routes: int32 [8192, 2], P(('expert', 'req')), may hold values from 0 to 3, all different within a row
- residual: bfloat16 [8192, 1024], P(('expert', 'req')), may hold values from -20 to 20
- w_attn_out: bfloat16 [1024, 1024], replicated, may hold values from -0.1875 to 0.1875
- gain_attn: bfloat16 [1024], replicated, may hold values from 0.25 to 1.75
- w_router: bfloat16 [1024, 4], replicated, may hold values from -0.1875 to 0.1875
- w_in: bfloat16 [4, 1024, 2816], P('expert'), may hold values from -0.1875 to 0.1875
- w_out: bfloat16 [4, 1408, 1024], P('expert'), may hold values from -0.15625 to 0.15625
- gain_out: bfloat16 [1024], replicated, may hold values from 0.25 to 1.75
Outputs:
- layer_out: bfloat16 [8192, 1024], P(('expert', 'req'))
Inputs may be any that keep to these rules, and one draw needn't show every extreme that they name: Each row of page_table is a permutation of 0 to 7.
All inputs are finite; a program needn't handle non-finite values.
Results may differ from a plain program's by a relative error of at most 0.01.
Values may be sent and summed in bfloat16 or wider, within the bound.
A program may use at most 128 MiB of HBM per device.

v0:
```python
import math
import jax
import jax.numpy as jnp
from jax import lax
from jax.sharding import PartitionSpec as P

HEADS = 16
HEAD_DIM = 64
TOP = 2
PAGE = 128
HD = 1024
norm_eps = 1e-06


def block_size(total_count, largest):
    chosen = min(total_count, largest)
    while total_count % chosen:
        chosen -= 1
    return chosen


def key_positions(table_row, key_count, page_len):
    logical = jnp.arange(table_row.shape[0], dtype=jnp.int32)
    inverse = jnp.sum(
        jnp.where(table_row[:, None] == logical[None, :], logical[:, None], 0), axis=0
    )
    flat_index = jnp.arange(key_count, dtype=jnp.int32)
    page_index = flat_index // page_len
    logical_page = jnp.sum(
        jnp.where(page_index[:, None] == logical[None, :], inverse[None, :], 0), axis=1
    )
    return logical_page * page_len + flat_index % page_len


def rms_scale(values, gain_row):
    mean_square = jnp.mean(values * values, axis=-1, keepdims=True)
    return values * lax.rsqrt(mean_square + norm_eps) * gain_row.astype(jnp.float32)


def route_block(route_rows, cap_size, expert_count):
    onehot = (
        route_rows[:, :, None] == jnp.arange(expert_count, dtype=jnp.int32)[None, None, :]
    ).astype(jnp.int32)
    ordered = onehot.transpose(1, 0, 2).reshape(-1, expert_count)
    earlier = jnp.cumsum(ordered, axis=0) - ordered
    position = jnp.sum(earlier * ordered, axis=1).reshape(route_rows.shape[1], route_rows.shape[0])
    kept_mask = position < cap_size
    slot_ids = jnp.where(kept_mask, route_rows.T * cap_size + position, -1)
    return (onehot, kept_mask, slot_ids)


def on_device(
    queries,
    self_kv,
    kv_pages,
    page_table,
    lengths,
    routes,
    residual,
    w_attn_out,
    gain_attn,
    w_router,
    w_in,
    w_out,
    gain_out,
):
    row_count = queries.shape[0]
    scale_qk = 1.0 / math.sqrt(HEAD_DIM)
    table_row = page_table[0]
    page_rows = kv_pages.reshape(-1, kv_pages.shape[-1])
    query_h = queries.reshape(row_count, HEADS, HEAD_DIM)
    own_key = self_kv[:, :HD].reshape(row_count, HEADS, HEAD_DIM)
    own_value = self_kv[:, HD:].reshape(row_count, HEADS, HEAD_DIM)
    own_score = (
        jnp.einsum("rhd,rhd->hr", query_h, own_key, preferred_element_type=jnp.float32) * scale_qk
    )
    start_value = jnp.swapaxes(own_value, 0, 1).astype(jnp.float32)
    initial = (own_score, jnp.ones_like(own_score), start_value)
    page_piece = lax.all_gather(page_rows, "req", axis=0, tiled=True)
    piece_len = page_piece.shape[0]
    step_len = block_size(piece_len, 512)
    positions = key_positions(table_row, piece_len, PAGE)
    blocks = page_piece.reshape(piece_len // step_len, step_len, page_piece.shape[1])
    block_pos = positions.reshape(piece_len // step_len, step_len)

    def add_block(running, block_items):
        highest, weight_sum, weighted = running
        block_rows, block_place = block_items
        key_rows = block_rows[:, :HD].reshape(step_len, HEADS, HEAD_DIM)
        value_rows = block_rows[:, HD:].reshape(step_len, HEADS, HEAD_DIM)
        scores = (
            jnp.einsum("rhd,khd->hrk", query_h, key_rows, preferred_element_type=jnp.float32)
            * scale_qk
        )
        visible = block_place[None, :] < lengths[:, None]
        masked = jnp.where(visible[None], scores, -jnp.inf)
        new_high = jnp.maximum(highest, jnp.max(masked, axis=2))
        factor = jnp.exp(highest - new_high)
        weights = jnp.exp(masked - new_high[:, :, None])
        weight_sum = weight_sum * factor + jnp.sum(weights, axis=2)
        weighted = weighted * factor[:, :, None] + jnp.einsum(
            "hrk,khd->hrd",
            weights.astype(jnp.bfloat16),
            value_rows,
            preferred_element_type=jnp.float32,
        )
        return ((new_high, weight_sum, weighted), None)

    result, unused = lax.scan(add_block, initial, (blocks, block_pos))
    highest, weight_sum, weighted = result
    attended = (
        (weighted / weight_sum[:, :, None])
        .transpose(1, 0, 2)
        .reshape(row_count, HD)
        .astype(jnp.bfloat16)
    )
    residual_sum = residual.astype(jnp.float32) + jnp.dot(
        attended, w_attn_out, preferred_element_type=jnp.float32
    )
    normed = rms_scale(residual_sum, gain_attn).astype(jnp.bfloat16)
    logits = jnp.dot(normed, w_router, preferred_element_type=jnp.float32)
    experts_all = w_router.shape[1]
    cap_size = (5 * row_count * TOP + 4 * experts_all - 1) // (4 * experts_all)
    onehot, kept_mask, slot_ids = route_block(routes, cap_size, experts_all)
    picked = jnp.sum(jnp.where(onehot > 0, logits[:, None, :], 0.0), axis=2)
    gate_values = jax.nn.sigmoid(picked - picked[:, ::-1])
    slot_range = jnp.arange(experts_all * cap_size, dtype=jnp.int32)
    assign = jnp.sum(
        (slot_ids[:, None, :] == slot_range[None, :, None]).astype(jnp.bfloat16), axis=0
    )
    model_width = normed.shape[1]
    buffer = (
        jnp.dot(assign, normed, preferred_element_type=jnp.float32)
        .astype(jnp.bfloat16)
        .reshape(experts_all, cap_size, model_width)
    )
    arrived = lax.all_to_all(buffer, "expert", split_axis=0, concat_axis=0, tiled=True)
    slot_count = arrived.shape[1]
    local_experts = w_in.shape[0]
    hidden_width = w_out.shape[1]
    grouped = arrived.reshape(-1, local_experts, slot_count, model_width)
    inner_act = jnp.einsum("slnd,ldf->slnf", grouped, w_in, preferred_element_type=jnp.float32)
    hidden = (
        jax.nn.gelu(inner_act[..., :hidden_width], approximate=True) * inner_act[..., hidden_width:]
    ).astype(jnp.bfloat16)
    outcome = jnp.einsum(
        "slnf,lfd->slnd", hidden, w_out, preferred_element_type=jnp.float32
    ).astype(jnp.bfloat16)
    expert_done = outcome.reshape(-1, slot_count, model_width)
    collected = lax.all_to_all(expert_done, "expert", split_axis=0, concat_axis=0, tiled=True)
    flat_rows = collected.reshape(-1, model_width)
    picked_rows = flat_rows[jnp.maximum(slot_ids, 0)]
    gate_kept = jnp.where(kept_mask, gate_values.T, 0.0)
    mixture = jnp.sum(picked_rows.astype(jnp.float32) * gate_kept[:, :, None], axis=0)
    return rms_scale(residual_sum + mixture, gain_out).astype(jnp.bfloat16)


def solution(mesh):
    in_specs = (
        P(("expert", "req"), None),
        P(("expert", "req"), None),
        P(("expert", "req"), None, None),
        P("expert", None),
        P(("expert", "req")),
        P(("expert", "req"), None),
        P(("expert", "req"), None),
        P(),
        P(),
        P(),
        P("expert", None, None),
        P("expert", None, None),
        P(),
    )
    out_specs = P(("expert", "req"), None)
    return jax.shard_map(
        on_device, mesh=mesh, in_specs=in_specs, out_specs=out_specs, check_vma=False
    )
```

profile of v0, /device:TPU:0, one launch (start us, length us, event | category | flops | bytes accessed | tf_op | source)
XLA Modules:
  0.0 183.3 jit_solution(17256257046171117510)
XLA Ops:
  7.3 2.5 %slice_convert_fusion = (f32[256,1024]{1,0:T(8,128)}, bf16[256,1024]{1,0:T(8,128)(2,1)S(1)}) fusion(bf16[256,2048]{1,0:T(8,128)(2,1)} %param.16), kind=kLoop, calls=%fused_computation.51 | loop fusion | flops 262144 | bytes 2621440 | tf_op jit(solution)/shard_map/convert_element_type | solution.py:77
  12.0 2.6 %copy.29 = f32[256,1024]{0,1:T(8,128)} copy(f32[256,1024]{1,0:T(8,128)} %get-tuple-element.119) | data formatting | bytes 2097152 | tf_op jit(solution)/shard_map/convert_element_type | solution.py:77
  21.2 37.7 %all-gather.3.cloned.1.call-done = bf16[1,1024,2048]{2,1,0:T(8,128)(2,1)} async-done(((bf16[1,128,2048]{2,1,0:T(8,128)(2,1)}), bf16[1,1024,2048]{2,1,0:T(8,128)(2,1)}) %all-gather.3.cloned.1.call-update) | async-done | bytes 4194320 | tf_op jit(solution)/shard_map/all_gather | solution.py:79
  58.9 54.3 %while.15 = (s32[]{:T(128)}, f32[16,256]{1,0:T(8,128)}, f32[16,256]{1,0:T(8,128)}, f32[16,256,64]{1,2,0:T(8,128)}, s32[2,512]{1,0:T(2,128)}, /*index=5*/s32[256]...) while((s32[]{:T(128)}, f32[16,256]{1,0:T(8,128)}, ...), condition=%wide.region_5.6_spmd.clone, body=%wide.region_2.5_spmd.clone.sunk | while | flops 560607232 | bytes 76881064 | solution.py:109
  60.4 3.1 %constant_dynamic-slice_fusion.5 = bf16[1,512,2048]{2,1,0:T(8,128)(2,1)} fusion(bf16[2,512,2048]{2,1,0:T(8,128)(2,1)} %get-tuple-element.210, s32[]{:T(128)} %get-tuple-element.194), kind=kLoop, calls=%fused_computation.13.clone.1 | loop fusion | bytes 4194308 | tf_op jit(solution)/shard_map/while/body/jit(dynamic_index_in_dim)/dynamic_slice | solution.py:109
  63.5 3.9 %copy.48 = bf16[1,512,2048]{1,2,0:T(8,128)(2,1)} copy(bf16[1,512,2048]{2,1,0:T(8,128)(2,1)} %constant_dynamic-slice_fusion.5) | data formatting | bytes 4194304 | tf_op jit(solution)/shard_map/while/body/jit(dynamic_index_in_dim)/dynamic_slice | solution.py:109
  67.4 2.6 %fusion.78 = (bf16[512,1024]{0,1:T(8,128)(2,1)}, bf16[512,1024]{0,1:T(8,128)(2,1)S(1)}) fusion(bf16[512,2048]{0,1:T(8,128)(2,1)} %bitcast.117), kind=kLoop, calls=%fused_computation.94.clone.1 | loop fusion | bytes 4194304 | tf_op jit(solution)/shard_map/while/body/eval_jaxpr/slice | solution.py:90
  71.6 3.2 %copy-done.1 = f32[16,512,256]{2,1,0:T(8,128)} copy-done((f32[16,512,256]{2,1,0:T(8,128)}, f32[16,512,256]{2,1,0:T(8,128)S(1)}, u32[]{:S(2)}) %copy-start.1) | copy-done | bytes 8388632 | tf_op jit(solution)/shard_map/while
  74.8 2.3 %fusion.80 = f32[16,256]{1,0:T(8,128)} fusion(f32[16,512,256]{2,1,0:T(8,128)S(1)} %get-tuple-element.180, f32[16,256]{1,0:T(8,128)S(1)} %max.10, pred[256,512]{0,1:T(8,128)(4,1)S(1)} %broadcast_compare_fusion.3), kind=kLoop, calls=%fused_computation.4.clone.1 | loop fusion | flops 8384512 | bytes 8552448 | tf_op jit(solution)/shard_map/while/body/eval_jaxpr/reduce_sum | solution.py:100
  78.4 7.0 %fusion.82 = f32[16,256,64]{1,2,0:T(8,128)} fusion(bf16[512,16,64]{0,2,1:T(8,128)(2,1)} %bitcast.120, f32[16,512,256]{2,1,0:T(8,128)} %copy-done.1, f32[16,256]{1,0:T(8,128)S(1)} %max.10, pred[256,512]{0,1:T(8,128)(4,1)S(1)} %broadcast_compare_fusion.3, f32[16,256,64]{1,2,0:T(8,128)} %get-tuple-element.197, f32[16,256]{1,0:T(8,128)S(1)} %get-tuple-element.183), kind=kOutput, calls=%fused_computation.8.clone.1 | convolution fusion | flops 277348352 | bytes 11698176 | tf_op jit(solution)/shard_map/while/body/eval_jaxpr/hrk,khd->hrd/dot_general | solution.py:101
  87.5 3.1 %constant_dynamic-slice_fusion.5 = bf16[1,512,2048]{2,1,0:T(8,128)(2,1)} fusion(bf16[2,512,2048]{2,1,0:T(8,128)(2,1)} %get-tuple-element.210, s32[]{:T(128)} %get-tuple-element.194), kind=kLoop, calls=%fused_computation.13.clone.1 | loop fusion | bytes 4194308 | tf_op jit(solution)/shard_map/while/body/jit(dynamic_index_in_dim)/dynamic_slice | solution.py:109
  90.7 3.9 %copy.48 = bf16[1,512,2048]{1,2,0:T(8,128)(2,1)} copy(bf16[1,512,2048]{2,1,0:T(8,128)(2,1)} %constant_dynamic-slice_fusion.5) | data formatting | bytes 4194304 | tf_op jit(solution)/shard_map/while/body/jit(dynamic_index_in_dim)/dynamic_slice | solution.py:109
  94.6 2.6 %fusion.78 = (bf16[512,1024]{0,1:T(8,128)(2,1)}, bf16[512,1024]{0,1:T(8,128)(2,1)S(1)}) fusion(bf16[512,2048]{0,1:T(8,128)(2,1)} %bitcast.117), kind=kLoop, calls=%fused_computation.94.clone.1 | loop fusion | bytes 4194304 | tf_op jit(solution)/shard_map/while/body/eval_jaxpr/slice | solution.py:90
  98.8 3.2 %copy-done.1 = f32[16,512,256]{2,1,0:T(8,128)} copy-done((f32[16,512,256]{2,1,0:T(8,128)}, f32[16,512,256]{2,1,0:T(8,128)S(1)}, u32[]{:S(2)}) %copy-start.1) | copy-done | bytes 8388632 | tf_op jit(solution)/shard_map/while
  102.0 2.3 %fusion.80 = f32[16,256]{1,0:T(8,128)} fusion(f32[16,512,256]{2,1,0:T(8,128)S(1)} %get-tuple-element.180, f32[16,256]{1,0:T(8,128)S(1)} %max.10, pred[256,512]{0,1:T(8,128)(4,1)S(1)} %broadcast_compare_fusion.3), kind=kLoop, calls=%fused_computation.4.clone.1 | loop fusion | flops 8384512 | bytes 8552448 | tf_op jit(solution)/shard_map/while/body/eval_jaxpr/reduce_sum | solution.py:100
  105.6 7.0 %fusion.82 = f32[16,256,64]{1,2,0:T(8,128)} fusion(bf16[512,16,64]{0,2,1:T(8,128)(2,1)} %bitcast.120, f32[16,512,256]{2,1,0:T(8,128)} %copy-done.1, f32[16,256]{1,0:T(8,128)S(1)} %max.10, pred[256,512]{0,1:T(8,128)(4,1)S(1)} %broadcast_compare_fusion.3, f32[16,256,64]{1,2,0:T(8,128)} %get-tuple-element.197, f32[16,256]{1,0:T(8,128)S(1)} %get-tuple-element.183), kind=kOutput, calls=%fused_computation.8.clone.1 | convolution fusion | flops 277348352 | bytes 11698176 | tf_op jit(solution)/shard_map/while/body/eval_jaxpr/hrk,khd->hrd/dot_general | solution.py:101
  114.7 2.7 %multiply_reduce_fusion.1 = (f32[256]{0:T(256)S(1)}, f32[256,1024]{1,0:T(8,128)S(1)}) fusion(bf16[256,1024]{0,1:T(8,128)(2,1)S(1)} %bitcast.125, bf16[1024,1024]{1,0:T(8,128)(2,1)} %param.22, bf16[256,1024]{1,0:T(8,128)(2,1)} %param.21), kind=kOutput, calls=%fused_computation.48 | convolution fusion | flops 537919232 | bytes 4195328 | tf_op jit(solution)/shard_map/dot_general | solution.py:117
  119.0 20.8 %all_to_all.10 = bf16[4,160,1024]{2,1,0:T(8,128)(2,1)S(1)} all-to-all(bf16[4,160,1024]{2,1,0:T(8,128)(2,1)S(1)} %bitcast.122), channel_id=1, replica_groups=mesh['expert'=4,'req'=8] {'expert'}, dimensions={0} | all-to-all | bytes 2621440 | tf_op jit(solution)/shard_map/all_to_all | solution.py:137
  139.8 3.9 %fusion.14 = f32[4,1,160,2816]{3,2,0,1:T(8,128)S(1)} fusion(bf16[4,160,1024]{2,1,0:T(8,128)(2,1)S(1)} %all_to_all.10, bf16[1,1024,2816]{2,1,0:T(8,128)(2,1)S(1)} %bitcast.133), kind=kOutput, calls=%fused_computation.20 | convolution fusion | flops 3690987520 | bytes 14286848 | tf_op jit(solution)/shard_map/slnd,ldf->slnf/dot_general | solution.py:142
  143.7 3.6 %fusion.34 = bf16[4,160,1024]{2,1,0:T(8,128)(2,1)} fusion(bf16[1,1408,1024]{2,1,0:T(8,128)(2,1)S(1)} %copy-done, f32[4,1,160,2816]{3,2,0,1:T(8,128)S(1)} %fusion.14), kind=kOutput, calls=%fused_computation.39 | convolution fusion | flops 1855160320 | bytes 11403264 | tf_op jit(solution)/shard_map/slnf,lfd->slnd/dot_general | solution.py:146
  147.4 4.4 %all-to-all-start.1 = ((bf16[4,160,1024]{2,1,0:T(8,128)(2,1)}), bf16[4,160,1024]{2,1,0:T(8,128)(2,1)}, u32[]{:S(2)}, u32[]{:S(2)}) async-start(bf16[4,160,1024]{2,1,0:T(8,128)(2,1)} %fusion.34), calls=%async_computation.1 | async-start | bytes 2621440 | tf_op jit(solution)/shard_map/all_to_all | solution.py:150
  153.6 13.9 %all-to-all-done.1 = bf16[4,160,1024]{2,1,0:T(8,128)(2,1)} async-done(((bf16[4,160,1024]{2,1,0:T(8,128)(2,1)}), bf16[4,160,1024]{2,1,0:T(8,128)(2,1)}, u32[]{:S(2)}, u32[]{:S(2)}) %all-to-all-start.1) | async-done | bytes 1310752 | tf_op jit(solution)/shard_map/all_to_all | solution.py:150
  167.5 5.0 %gather_fusion = bf16[512,1024]{1,0:T(8,128)(2,1)} fusion(bf16[640,1024]{1,0:T(8,128)(2,1)} %bitcast.26, s32[1024]{0:T(1024)S(1)} %pad_clamp_fusion), kind=kCustom, calls=%fused_computation | custom fusion | bytes 2099200 | tf_op jit(solution)/shard_map/gather | solution.py:152
  172.5 1.6 fusion.28
  (87 shorter events, 26.6 us)
Async XLA Ops:
  6.5 137.2 %copy-start = (bf16[1,1408,1024]{2,1,0:T(8,128)(2,1)S(1)}, bf16[1,1408,1024]{2,1,0:T(8,128)(2,1)}, u32[]{:S(2)}) copy-start(bf16[1,1408,1024]{2,1,0:T(8,128)(2,1)} %param.26) | copy-start | bytes 8650756
  6.5 8.1 %copy-start.14 = (s32[1,8]{1,0:T(1,128)S(1)}, s32[1,8]{1,0:T(1,128)}, u32[]{:S(2)}) copy-start(s32[1,8]{1,0:T(1,128)} %param.18) | copy-start | bytes 100
  6.5 8.3 %copy-start.12 = (bf16[1024]{0:T(1024)(128)(2,1)S(1)}, bf16[1024]{0:T(1024)(128)(2,1)}, u32[]{:S(2)}) copy-start(bf16[1024]{0:T(1024)(128)(2,1)} %param.23) | copy-start | bytes 6148
  6.5 8.8 %copy-start.6 = (s32[256,2]{0,1:T(2,128)S(1)}, s32[256,2]{0,1:T(2,128)}, u32[]{:S(2)}) copy-start(s32[256,2]{0,1:T(2,128)} %param.20) | copy-start | bytes 6148
  6.5 52.3 %all-gather.3.cloned.1.call-start = ((), (), s32[]{:S(2)}) async-start(), calls=%async_computation.2 | async-start | bytes 4718592 | tf_op jit(solution)/shard_map/all_gather | solution.py:79
  17.1 41.7 %copy-start.8 = (s32[2,256]{1,0:T(2,128)}, s32[2,256]{1,0:T(2,128)S(1)}, u32[]{:S(2)}) copy-start(s32[2,256]{1,0:T(2,128)S(1)} %reshape.142) | copy-start | bytes 6148
  70.1 1.5 copy-start.3
  71.6 3.2 %copy-start.1 = (f32[16,512,256]{2,1,0:T(8,128)}, f32[16,512,256]{2,1,0:T(8,128)S(1)}, u32[]{:S(2)}) copy-start(f32[16,512,256]{2,1,0:T(8,128)S(1)} %get-tuple-element.180) | copy-start | bytes 25165828 | tf_op jit(solution)/shard_map/while
  97.2 1.5 copy-start.3
  98.7 3.2 %copy-start.1 = (f32[16,512,256]{2,1,0:T(8,128)}, f32[16,512,256]{2,1,0:T(8,128)S(1)}, u32[]{:S(2)}) copy-start(f32[16,512,256]{2,1,0:T(8,128)S(1)} %get-tuple-element.180) | copy-start | bytes 25165828 | tf_op jit(solution)/shard_map/while
  113.2 5.2 %copy-start.4 = (bf16[640,256]{1,0:T(8,128)(2,1)S(1)}, bf16[640,256]{1,0:T(8,128)(2,1)}, u32[]{:S(2)}) copy-start(bf16[640,256]{1,0:T(8,128)(2,1)} %fusion.41) | copy-start | bytes 983044
  113.2 5.2 %copy-start.5 = (f32[1024]{0:T(1024)S(1)}, f32[1024]{0:T(1024)}, u32[]{:S(2)}) copy-start(f32[1024]{0:T(1024)} %convert_element_type.77) | copy-start | bytes 12292
  113.2 26.6 %slice-start = ((s8[5767168]{0:T(1024)(128)(4,1)}), s8[4194304]{0:T(1024)(128)(4,1)S(1)}, s32[]{:S(2)}) async-start(s8[5767168]{0:T(1024)(128)(4,1)} %bitcast.132), calls=%async_computation.3 | async-start | bytes 8388608
  114.7 25.1 %slice-start.1 = ((s8[5767168]{0:T(1024)(128)(4,1)}), s8[1572864]{0:T(1024)(128)(4,1)S(1)}, s32[]{:S(2)}) async-start(s8[5767168]{0:T(1024)(128)(4,1)} %bitcast.132), calls=%async_computation.4 | async-start | bytes 3145728
  117.4 1.0 copy-start.2
  143.7 8.1 %copy-start.11 = (s32[1,2,2,128]{3,2,1,0:T(2,128)S(1)}, s32[1,2,2,128]{3,2,1,0:T(2,128)}, u32[]{:S(2)}) copy-start(s32[1,2,2,128]{3,2,1,0:T(2,128)} %get-tuple-element.113) | copy-start | bytes 6148
  143.7 8.1 %copy-start.13 = (bf16[1024]{0:T(1024)(128)(2,1)S(1)}, bf16[1024]{0:T(1024)(128)(2,1)}, u32[]{:S(2)}) copy-start(bf16[1024]{0:T(1024)(128)(2,1)} %param.27) | copy-start | bytes 6148
  143.7 8.1 %copy-start.10 = (bf16[1024,4]{0,1:T(4,128)(2,1)S(1)}, bf16[1024,4]{0,1:T(4,128)(2,1)}, u32[]{:S(2)}) copy-start(bf16[1024,4]{0,1:T(4,128)(2,1)} %param.24) | copy-start | bytes 24580
  147.4 6.0 %copy-start.7 = (s32[256,2]{0,1:T(2,128)S(1)}, s32[256,2]{0,1:T(2,128)}, u32[]{:S(2)}) copy-start(s32[256,2]{0,1:T(2,128)} %param.20) | copy-start | bytes 6148
  147.4 6.1 %copy-start.9 = (s32[2,256]{1,0:T(2,128)S(1)}, s32[2,256]{1,0:T(2,128)}, u32[]{:S(2)}) copy-start(s32[2,256]{1,0:T(2,128)} %copy-done.8) | copy-start | bytes 6148
  147.4 20.1 %all-to-all-start.1 = ((bf16[4,160,1024]{2,1,0:T(8,128)(2,1)}), bf16[4,160,1024]{2,1,0:T(8,128)(2,1)}, u32[]{:S(2)}, u32[]{:S(2)}) async-start(bf16[4,160,1024]{2,1,0:T(8,128)(2,1)} %fusion.34), calls=%async_computation.1 | async-start | bytes 2621440 | tf_op jit(solution)/shard_map/all_to_all | solution.py:150
Sparse Core Ops, SparseCore 0:
  9.0 49.8 all-gather.2
where the time goes:
time: 184 us; the launch traced here: 183 us
  waiting for transfers between devices  52.3 us (28%)
  local copies, waits for them, and re-layouts  39.6 us (22%)
  matrix products  29.3 us (16%)
  other arithmetic  23.2 us (13%)
  blocking collectives  20.8 us (11%)
  between operations  13.6 us (7%)
  starting transfers between devices  4.44 us (2%)
    all_gather x1, waiting for transfers between devices, on_device(): page_piece = lax.all_gather(page_rows, 'req', axis=0, tiled=True)  37.7 us
    all_to_all x1, blocking collectives, on_device(): lax.all_to_all(buffer, 'expert', split_axis=0, concat_axis=0, tiled=True)  20.8 us
    dynamic_slice x6, local copies, waits for them, and re-layouts, on_device(): result, unused = lax.scan(add_block, initial, (blocks, block_pos))  15.5 us
    dot_general x2, matrix products, add_block(): jnp.einsum('hrk,khd->hrd', weights.astype(jnp.bfloat16), value_rows, pref...  14 us
    all_to_all x1, waiting for transfers between devices, on_device(): lax.all_to_all(expert_done, 'expert', split_axis=0, concat_axis=0, tiled=...  13.9 us
    while x10, local copies, waits for them, and re-layouts  7.6 us
    slice x2, local copies, waits for them, and re-layouts, add_block(): value_rows = block_rows[:, HD:].reshape(step_len, HEADS, HEAD_DIM)  5.29 us
    gather x1, local copies, waits for them, and re-layouts, on_device(): picked_rows = flat_rows[jnp.maximum(slot_ids, 0)]  4.97 us
  transfers between devices with their start and end apart: 2, of which 2 were waited for; matrix products, arithmetic and copies ran while one was open for 8% of the time, Pallas kernels for 0%

commit v1 on v0

--- a/solution.py
+++ b/solution.py
@@ -76,7 +76,31 @@
     )
     start_value = jnp.swapaxes(own_value, 0, 1).astype(jnp.float32)
     initial = (own_score, jnp.ones_like(own_score), start_value)
-    page_piece = lax.all_gather(page_rows, "req", axis=0, tiled=True)
+    outcome_arr, mid_arr, b_now = (lax.axis_size("req"), lax.axis_index("req"), page_rows.shape[0])
+    page_piece = lax.dynamic_update_slice_in_dim(
+        jnp.zeros(
+            [k * outcome_arr if nth == 0 else k for nth, k in enumerate(page_rows.shape)],
+            page_rows.dtype,
+        ),
+        page_rows,
+        mid_arr * b_now,
+        axis=0,
+    )
+    heard = m_next = page_rows
+    for hop_no in range(1, outcome_arr // 2 + 1):
+        heard = lax.ppermute(
+            heard, "req", [(nth, (nth + 1) % outcome_arr) for nth in range(outcome_arr)]
+        )
+        page_piece = lax.dynamic_update_slice_in_dim(
+            page_piece, heard, (mid_arr - hop_no) % outcome_arr * b_now, axis=0
+        )
+        if 2 * hop_no < outcome_arr:
+            m_next = lax.ppermute(
+                m_next, "req", [(nth, (nth - 1) % outcome_arr) for nth in range(outcome_arr)]
+            )
+            page_piece = lax.dynamic_update_slice_in_dim(
+                page_piece, m_next, (mid_arr + hop_no) % outcome_arr * b_now, axis=0
+            )
     piece_len = page_piece.shape[0]
     step_len = block_size(piece_len, 512)
     positions = key_positions(table_row, piece_len, PAGE)

time: 184 us -> 169 us (0.918)
  the two profiles are of different devices: /device:TPU:0 before, /device:TPU:8 now
where the time goes in v1:
time: 169 us; the launch traced here: 168 us
  local copies, waits for them, and re-layouts  53.1 us (31%)
  matrix products  29.3 us (17%)
  waiting for transfers between devices  25.2 us (15%)
  other arithmetic  23 us (14%)
  blocking collectives  22 us (13%)
  starting transfers between devices  15.2 us (9%)
    all_to_all x1, blocking collectives, on_device(): lax.all_to_all(buffer, 'expert', split_axis=0, concat_axis=0, tiled=True)  22 us
    dynamic_slice x6, local copies, waits for them, and re-layouts, on_device(): result, unused = lax.scan(add_block, initial, (blocks, block_pos))  15.5 us
    all_to_all x1, waiting for transfers between devices, on_device(): lax.all_to_all(expert_done, 'expert', split_axis=0, concat_axis=0, tiled=...  15.3 us
    dot_general x2, matrix products, add_block(): jnp.einsum('hrk,khd->hrd', weights.astype(jnp.bfloat16), value_rows, pref...  14 us
    ppermute x4, waiting for transfers between devices, on_device(): lax.ppermute(heard, 'req', [(nth, (nth + 1) % outcome_arr) for nth in ran...  8.47 us
    while x10, local copies, waits for them, and re-layouts  7.59 us
    ppermute x4, starting transfers between devices, on_device(): lax.ppermute(heard, 'req', [(nth, (nth + 1) % outcome_arr) for nth in ran...  7.37 us
    dynamic_update_slice x4, local copies, waits for them, and re-layouts, on_device(): lax.dynamic_update_slice_in_dim(page_piece, heard, (mid_arr - hop_no) % o...  5.56 us
  transfers between devices with their start and end apart: 8, of which 5 were waited for; matrix products, arithmetic and copies ran while one was open for 17% of the time, Pallas kernels for 0%

profile of v1, /device:TPU:8, one launch (start us, length us, event | category | flops | bytes accessed | tf_op | source)
XLA Modules:
  0.0 168.2 jit_solution(13422913978136165710)
XLA Ops:
  1.8 2.3 %slice_convert_fusion = (f32[256,1024]{1,0:T(8,128)}, bf16[256,1024]{1,0:T(8,128)(2,1)S(1)}) fusion(bf16[256,2048]{1,0:T(8,128)(2,1)} %param.16), kind=kLoop, calls=%fused_computation.51 | loop fusion | flops 262144 | bytes 2621440 | tf_op jit(solution)/shard_map/convert_element_type | solution.py:77
  12.4 2.5 %broadcast_in_dim.91 = bf16[1024,2048]{1,0:T(8,128)(2,1)} broadcast(bf16[]{:T(256)} %constant.115.clone.1), dimensions={} | broadcast | bytes 4194306 | tf_op jit(solution)/shard_map/broadcast_in_dim | solution.py:81
  18.6 2.6 %copy.29 = f32[256,1024]{0,1:T(8,128)} copy(f32[256,1024]{1,0:T(8,128)} %get-tuple-element.119) | data formatting | bytes 2097152 | tf_op jit(solution)/shard_map/convert_element_type | solution.py:77
  21.8 4.6 %collective-permute-start.4 = (bf16[128,2048]{1,0:T(8,128)(2,1)}, bf16[128,2048]{1,0:T(8,128)(2,1)S(1)}, u32[]{:S(2)}, u32[]{:S(2)}) collective-permute-start(bf16[128,2048]{1,0:T(8,128)(2,1)} %collective-permute-done.2), channel_id=1, source_target_pairs={{0,1},{1,2},{2,3},{3,4},{4,5},{5,6},{6,7},{7,0},{8,9},{9,10},{10,1... | collective-permute-start | bytes 1572872 | tf_op jit(solution)/shard_map/ppermute | solution.py:91
  33.6 2.7 %collective-permute-start.6 = (bf16[128,2048]{1,0:T(8,128)(2,1)S(1)}, bf16[128,2048]{1,0:T(8,128)(2,1)S(1)}, u32[]{:S(2)}, u32[]{:S(2)}) collective-permute-start(bf16[128,2048]{1,0:T(8,128)(2,1)S(1)} %collective-permute-done.4), channel_id=1, source_target_pairs={{0,1},{1,2},{2,3},{3,4},{4,5},{5,6},{6,7},{7,0},{8,9},{9,10},{10,1... | collective-permute-start | bytes 1572872 | tf_op jit(solution)/shard_map/ppermute | solution.py:91
  41.3 6.0 %collective-permute-done.6 = bf16[128,2048]{1,0:T(8,128)(2,1)S(1)} collective-permute-done((bf16[128,2048]{1,0:T(8,128)(2,1)S(1)}, bf16[128,2048]{1,0:T(8,128)(2,1)S(1)}, u32[]{:S(2)}, u32[]{:S(2)}) %collective-permute-start.6) | collective-permute-done | bytes 524320 | tf_op jit(solution)/shard_map/ppermute | solution.py:91
  48.1 54.4 %while.15 = (s32[]{:T(128)}, f32[16,256]{1,0:T(8,128)}, f32[16,256]{1,0:T(8,128)}, f32[16,256,64]{1,2,0:T(8,128)}, s32[2,512]{1,0:T(2,128)}, /*index=5*/s32[256]...) while((s32[]{:T(128)}, f32[16,256]{1,0:T(8,128)}, ...), condition=%wide.region_5.6_spmd.clone, body=%wide.region_2.5_spmd.clone.sunk | while | flops 560607232 | bytes 76881064 | solution.py:133
  49.7 3.1 %constant_dynamic-slice_fusion.5 = bf16[1,512,2048]{2,1,0:T(8,128)(2,1)} fusion(bf16[2,512,2048]{2,1,0:T(8,128)(2,1)} %get-tuple-element.210, s32[]{:T(128)} %get-tuple-element.194), kind=kLoop, calls=%fused_computation.13.clone.1 | loop fusion | bytes 4194308 | tf_op jit(solution)/shard_map/while/body/jit(dynamic_index_in_dim)/dynamic_slice | solution.py:133
  52.8 3.9 %copy.48 = bf16[1,512,2048]{1,2,0:T(8,128)(2,1)} copy(bf16[1,512,2048]{2,1,0:T(8,128)(2,1)} %constant_dynamic-slice_fusion.5) | data formatting | bytes 4194304 | tf_op jit(solution)/shard_map/while/body/jit(dynamic_index_in_dim)/dynamic_slice | solution.py:133
  56.7 2.6 %fusion.78 = (bf16[512,1024]{0,1:T(8,128)(2,1)}, bf16[512,1024]{0,1:T(8,128)(2,1)S(1)}) fusion(bf16[512,2048]{0,1:T(8,128)(2,1)} %bitcast.119), kind=kLoop, calls=%fused_computation.102.clone.1 | loop fusion | bytes 4194304 | tf_op jit(solution)/shard_map/while/body/eval_jaxpr/slice | solution.py:114
  60.9 3.2 %copy-done.1 = f32[16,512,256]{2,1,0:T(8,128)} copy-done((f32[16,512,256]{2,1,0:T(8,128)}, f32[16,512,256]{2,1,0:T(8,128)S(1)}, u32[]{:S(2)}) %copy-start.1) | copy-done | bytes 8388632 | tf_op jit(solution)/shard_map/while
  67.7 7.0 %fusion.82 = f32[16,256,64]{1,2,0:T(8,128)} fusion(bf16[512,16,64]{0,2,1:T(8,128)(2,1)} %bitcast.121, f32[16,512,256]{2,1,0:T(8,128)} %copy-done.1, f32[16,256]{1,0:T(8,128)S(1)} %max.10, pred[256,512]{0,1:T(8,128)(4,1)S(1)} %broadcast_compare_fusion.3, f32[16,256,64]{1,2,0:T(8,128)} %get-tuple-element.197, f32[16,256]{1,0:T(8,128)S(1)} %get-tuple-element.183), kind=kOutput, calls=%fused_computation.8.clone.1 | convolution fusion | flops 277348352 | bytes 11698176 | tf_op jit(solution)/shard_map/while/body/eval_jaxpr/hrk,khd->hrd/dot_general | solution.py:125
  76.8 3.1 %constant_dynamic-slice_fusion.5 = bf16[1,512,2048]{2,1,0:T(8,128)(2,1)} fusion(bf16[2,512,2048]{2,1,0:T(8,128)(2,1)} %get-tuple-element.210, s32[]{:T(128)} %get-tuple-element.194), kind=kLoop, calls=%fused_computation.13.clone.1 | loop fusion | bytes 4194308 | tf_op jit(solution)/shard_map/while/body/jit(dynamic_index_in_dim)/dynamic_slice | solution.py:133
  80.0 3.9 %copy.48 = bf16[1,512,2048]{1,2,0:T(8,128)(2,1)} copy(bf16[1,512,2048]{2,1,0:T(8,128)(2,1)} %constant_dynamic-slice_fusion.5) | data formatting | bytes 4194304 | tf_op jit(solution)/shard_map/while/body/jit(dynamic_index_in_dim)/dynamic_slice | solution.py:133
  83.9 2.6 %fusion.78 = (bf16[512,1024]{0,1:T(8,128)(2,1)}, bf16[512,1024]{0,1:T(8,128)(2,1)S(1)}) fusion(bf16[512,2048]{0,1:T(8,128)(2,1)} %bitcast.119), kind=kLoop, calls=%fused_computation.102.clone.1 | loop fusion | bytes 4194304 | tf_op jit(solution)/shard_map/while/body/eval_jaxpr/slice | solution.py:114
  88.1 3.2 %copy-done.1 = f32[16,512,256]{2,1,0:T(8,128)} copy-done((f32[16,512,256]{2,1,0:T(8,128)}, f32[16,512,256]{2,1,0:T(8,128)S(1)}, u32[]{:S(2)}) %copy-start.1) | copy-done | bytes 8388632 | tf_op jit(solution)/shard_map/while
  94.9 7.0 %fusion.82 = f32[16,256,64]{1,2,0:T(8,128)} fusion(bf16[512,16,64]{0,2,1:T(8,128)(2,1)} %bitcast.121, f32[16,512,256]{2,1,0:T(8,128)} %copy-done.1, f32[16,256]{1,0:T(8,128)S(1)} %max.10, pred[256,512]{0,1:T(8,128)(4,1)S(1)} %broadcast_compare_fusion.3, f32[16,256,64]{1,2,0:T(8,128)} %get-tuple-element.197, f32[16,256]{1,0:T(8,128)S(1)} %get-tuple-element.183), kind=kOutput, calls=%fused_computation.8.clone.1 | convolution fusion | flops 277348352 | bytes 11698176 | tf_op jit(solution)/shard_map/while/body/eval_jaxpr/hrk,khd->hrd/dot_general | solution.py:125
  104.0 2.7 %multiply_reduce_fusion.1 = (f32[256]{0:T(256)S(1)}, f32[256,1024]{1,0:T(8,128)S(1)}) fusion(bf16[256,1024]{0,1:T(8,128)(2,1)S(1)} %bitcast.126, bf16[1024,1024]{1,0:T(8,128)(2,1)} %param.22, bf16[256,1024]{1,0:T(8,128)(2,1)} %param.21), kind=kOutput, calls=%fused_computation.48 | convolution fusion | flops 537919232 | bytes 4195328 | tf_op jit(solution)/shard_map/dot_general | solution.py:141
  108.3 22.0 %all_to_all.10 = bf16[4,160,1024]{2,1,0:T(8,128)(2,1)S(1)} all-to-all(bf16[4,160,1024]{2,1,0:T(8,128)(2,1)S(1)} %bitcast.123), channel_id=1, replica_groups=mesh['expert'=4,'req'=8] {'expert'}, dimensions={0} | all-to-all | bytes 2621440 | tf_op jit(solution)/shard_map/all_to_all | solution.py:161
  130.3 3.9 %fusion.14 = f32[4,1,160,2816]{3,2,0,1:T(8,128)S(1)} fusion(bf16[4,160,1024]{2,1,0:T(8,128)(2,1)S(1)} %all_to_all.10, bf16[1,1024,2816]{2,1,0:T(8,128)(2,1)S(1)} %bitcast.136), kind=kOutput, calls=%fused_computation.20 | convolution fusion | flops 3690987520 | bytes 14286848 | tf_op jit(solution)/shard_map/slnd,ldf->slnf/dot_general | solution.py:166
  134.3 3.6 %fusion.34 = bf16[4,160,1024]{2,1,0:T(8,128)(2,1)} fusion(bf16[1,1408,1024]{2,1,0:T(8,128)(2,1)S(1)} %copy-done, f32[4,1,160,2816]{3,2,0,1:T(8,128)S(1)} %fusion.14), kind=kOutput, calls=%fused_computation.39 | convolution fusion | flops 1855160320 | bytes 11403264 | tf_op jit(solution)/shard_map/slnf,lfd->slnd/dot_general | solution.py:170
  137.9 4.3 %all-to-all-start.1 = ((bf16[4,160,1024]{2,1,0:T(8,128)(2,1)}), bf16[4,160,1024]{2,1,0:T(8,128)(2,1)}, u32[]{:S(2)}, u32[]{:S(2)}) async-start(bf16[4,160,1024]{2,1,0:T(8,128)(2,1)} %fusion.34), calls=%async_computation.1 | async-start | bytes 2621440 | tf_op jit(solution)/shard_map/all_to_all | solution.py:174
  143.9 15.3 %all-to-all-done.1 = bf16[4,160,1024]{2,1,0:T(8,128)(2,1)} async-done(((bf16[4,160,1024]{2,1,0:T(8,128)(2,1)}), bf16[4,160,1024]{2,1,0:T(8,128)(2,1)}, u32[]{:S(2)}, u32[]{:S(2)}) %all-to-all-start.1) | async-done | bytes 1310752 | tf_op jit(solution)/shard_map/all_to_all | solution.py:174
  159.3 5.0 %gather_fusion = bf16[512,1024]{1,0:T(8,128)(2,1)} fusion(bf16[640,1024]{1,0:T(8,128)(2,1)} %bitcast.27, s32[1024]{0:T(1024)S(1)} %pad_clamp_fusion), kind=kCustom, calls=%fused_computation | custom fusion | bytes 2099200 | tf_op jit(solution)/shard_map/gather | solution.py:176
  (109 shorter events, 50.5 us)
Async XLA Ops:
  0.0 134.2 %copy-start = (bf16[1,1408,1024]{2,1,0:T(8,128)(2,1)S(1)}, bf16[1,1408,1024]{2,1,0:T(8,128)(2,1)}, u32[]{:S(2)}) copy-start(bf16[1,1408,1024]{2,1,0:T(8,128)(2,1)} %param.26) | copy-start | bytes 8650756
  0.0 6.4 %copy-start.15 = (s32[1,8]{1,0:T(1,128)S(1)}, s32[1,8]{1,0:T(1,128)}, u32[]{:S(2)}) copy-start(s32[1,8]{1,0:T(1,128)} %param.18) | copy-start | bytes 100
  0.0 7.2 %copy-start.7 = (s32[256,2]{0,1:T(2,128)S(1)}, s32[256,2]{0,1:T(2,128)}, u32[]{:S(2)}) copy-start(s32[256,2]{0,1:T(2,128)} %param.20) | copy-start | bytes 6148
  0.0 12.4 %collective-permute-start = (bf16[128,2048]{1,0:T(8,128)(2,1)}, bf16[128,2048]{1,0:T(8,128)(2,1)}, u32[]{:S(2)}, u32[]{:S(2)}) collective-permute-start(bf16[128,2048]{1,0:T(8,128)(2,1)} %bitcast.127), channel_id=1, source_target_pairs={{0,1},{1,2},{2,3},{3,4},{4,5},{5,6},{6,7},{7,0},{8,9},{9,10},{10,1... | collective-permute-start | bytes 1572872 | tf_op jit(solution)/shard_map/ppermute | solution.py:91
  0.1 15.7 %collective-permute-start.1 = (bf16[128,2048]{1,0:T(8,128)(2,1)}, bf16[128,2048]{1,0:T(8,128)(2,1)}, u32[]{:S(2)}, u32[]{:S(2)}) collective-permute-start(bf16[128,2048]{1,0:T(8,128)(2,1)} %bitcast.128), channel_id=1, source_target_pairs={{0,7},{1,0},{2,1},{3,2},{4,3},{5,4},{6,5},{7,6},{8,15},{9,8},{10,9... | collective-permute-start | bytes 1572872 | tf_op jit(solution)/shard_map/ppermute | solution.py:98
  10.1 11.0 %copy-start.13 = (bf16[1024]{0:T(1024)(128)(2,1)S(1)}, bf16[1024]{0:T(1024)(128)(2,1)}, u32[]{:S(2)}) copy-start(bf16[1024]{0:T(1024)(128)(2,1)} %param.23) | copy-start | bytes 6148
  10.2 18.2 %copy-start.9 = (s32[2,256]{1,0:T(2,128)}, s32[2,256]{1,0:T(2,128)S(1)}, u32[]{:S(2)}) copy-start(s32[2,256]{1,0:T(2,128)S(1)} %reshape.142) | copy-start | bytes 6148
  11.4 3.6 %copy-start.5 = (bf16[1,128,2048]{2,1,0:T(8,128)(2,1)S(1)}, bf16[1,128,2048]{2,1,0:T(8,128)(2,1)}, u32[]{:S(2)}) copy-start(bf16[1,128,2048]{2,1,0:T(8,128)(2,1)} %param.17) | copy-start | bytes 1572868
  12.4 9.3 %collective-permute-start.2 = (bf16[128,2048]{1,0:T(8,128)(2,1)}, bf16[128,2048]{1,0:T(8,128)(2,1)}, u32[]{:S(2)}, u32[]{:S(2)}) collective-permute-start(bf16[128,2048]{1,0:T(8,128)(2,1)} %collective-permute-done), channel_id=1, source_target_pairs={{0,1},{1,2},{2,3},{3,4},{4,5},{5,6},{6,7},{7,0},{8,9},{9,10},{10,1... | collective-permute-start | bytes 1572872 | tf_op jit(solution)/shard_map/ppermute | solution.py:91
  15.8 14.5 %collective-permute-start.3 = (bf16[128,2048]{1,0:T(8,128)(2,1)}, bf16[128,2048]{1,0:T(8,128)(2,1)}, u32[]{:S(2)}, u32[]{:S(2)}) collective-permute-start(bf16[128,2048]{1,0:T(8,128)(2,1)} %collective-permute-done.1), channel_id=1, source_target_pairs={{0,7},{1,0},{2,1},{3,2},{4,3},{5,4},{6,5},{7,6},{8,15},{9,8},{10,9... | collective-permute-start | bytes 1572872 | tf_op jit(solution)/shard_map/ppermute | solution.py:98
  21.8 11.9 %collective-permute-start.4 = (bf16[128,2048]{1,0:T(8,128)(2,1)}, bf16[128,2048]{1,0:T(8,128)(2,1)S(1)}, u32[]{:S(2)}, u32[]{:S(2)}) collective-permute-start(bf16[128,2048]{1,0:T(8,128)(2,1)} %collective-permute-done.2), channel_id=1, source_target_pairs={{0,1},{1,2},{2,3},{3,4},{4,5},{5,6},{6,7},{7,0},{8,9},{9,10},{10,1... | collective-permute-start | bytes 1572872 | tf_op jit(solution)/shard_map/ppermute | solution.py:91
  30.2 10.2 %collective-permute-start.5 = (bf16[128,2048]{1,0:T(8,128)(2,1)}, bf16[128,2048]{1,0:T(8,128)(2,1)S(1)}, u32[]{:S(2)}, u32[]{:S(2)}) collective-permute-start(bf16[128,2048]{1,0:T(8,128)(2,1)} %collective-permute-done.3), channel_id=1, source_target_pairs={{0,7},{1,0},{2,1},{3,2},{4,3},{5,4},{6,5},{7,6},{8,15},{9,8},{10,9... | collective-permute-start | bytes 1572872 | tf_op jit(solution)/shard_map/ppermute | solution.py:98
  33.6 13.7 %collective-permute-start.6 = (bf16[128,2048]{1,0:T(8,128)(2,1)S(1)}, bf16[128,2048]{1,0:T(8,128)(2,1)S(1)}, u32[]{:S(2)}, u32[]{:S(2)}) collective-permute-start(bf16[128,2048]{1,0:T(8,128)(2,1)S(1)} %collective-permute-done.4), channel_id=1, source_target_pairs={{0,1},{1,2},{2,3},{3,4},{4,5},{5,6},{6,7},{7,0},{8,9},{9,10},{10,1... | collective-permute-start | bytes 1572872 | tf_op jit(solution)/shard_map/ppermute | solution.py:91
  88.0 3.2 %copy-start.1 = (f32[16,512,256]{2,1,0:T(8,128)}, f32[16,512,256]{2,1,0:T(8,128)S(1)}, u32[]{:S(2)}) copy-start(f32[16,512,256]{2,1,0:T(8,128)S(1)} %get-tuple-element.180) | copy-start | bytes 25165828 | tf_op jit(solution)/shard_map/while
  102.5 5.2 %copy-start.4 = (bf16[640,256]{1,0:T(8,128)(2,1)S(1)}, bf16[640,256]{1,0:T(8,128)(2,1)}, u32[]{:S(2)}) copy-start(bf16[640,256]{1,0:T(8,128)(2,1)} %fusion.41) | copy-start | bytes 983044
  102.5 5.2 %copy-start.6 = (f32[1024]{0:T(1024)S(1)}, f32[1024]{0:T(1024)}, u32[]{:S(2)}) copy-start(f32[1024]{0:T(1024)} %convert_element_type.77) | copy-start | bytes 12292
  102.5 27.8 %slice-start = ((s8[5767168]{0:T(1024)(128)(4,1)}), s8[4194304]{0:T(1024)(128)(4,1)S(1)}, s32[]{:S(2)}) async-start(s8[5767168]{0:T(1024)(128)(4,1)} %bitcast.135), calls=%async_computation.2 | async-start | bytes 8388608
  104.0 26.3 %slice-start.1 = ((s8[5767168]{0:T(1024)(128)(4,1)}), s8[1572864]{0:T(1024)(128)(4,1)S(1)}, s32[]{:S(2)}) async-start(s8[5767168]{0:T(1024)(128)(4,1)} %bitcast.135), calls=%async_computation.3 | async-start | bytes 3145728
  134.2 8.0 %copy-start.12 = (s32[1,2,2,128]{3,2,1,0:T(2,128)S(1)}, s32[1,2,2,128]{3,2,1,0:T(2,128)}, u32[]{:S(2)}) copy-start(s32[1,2,2,128]{3,2,1,0:T(2,128)} %get-tuple-element.113) | copy-start | bytes 6148
  134.2 8.0 %copy-start.14 = (bf16[1024]{0:T(1024)(128)(2,1)S(1)}, bf16[1024]{0:T(1024)(128)(2,1)}, u32[]{:S(2)}) copy-start(bf16[1024]{0:T(1024)(128)(2,1)} %param.27) | copy-start | bytes 6148
  134.2 8.0 %copy-start.11 = (bf16[1024,4]{0,1:T(4,128)(2,1)S(1)}, bf16[1024,4]{0,1:T(4,128)(2,1)}, u32[]{:S(2)}) copy-start(bf16[1024,4]{0,1:T(4,128)(2,1)} %param.24) | copy-start | bytes 24580
  134.2 9.6 %copy-start.8 = (s32[256,2]{0,1:T(2,128)S(1)}, s32[256,2]{0,1:T(2,128)}, u32[]{:S(2)}) copy-start(s32[256,2]{0,1:T(2,128)} %param.20) | copy-start | bytes 6148
  134.2 9.7 %copy-start.10 = (s32[2,256]{1,0:T(2,128)S(1)}, s32[2,256]{1,0:T(2,128)}, u32[]{:S(2)}) copy-start(s32[2,256]{1,0:T(2,128)} %copy-done.9) | copy-start | bytes 6148
  137.9 21.4 %all-to-all-start.1 = ((bf16[4,160,1024]{2,1,0:T(8,128)(2,1)}), bf16[4,160,1024]{2,1,0:T(8,128)(2,1)}, u32[]{:S(2)}, u32[]{:S(2)}) async-start(bf16[4,160,1024]{2,1,0:T(8,128)(2,1)} %fusion.34), calls=%async_computation.1 | async-start | bytes 2621440 | tf_op jit(solution)/shard_map/all_to_all | solution.py:174
  (4 other events, 7.2 us)
